TPU v7x, 256 devices: a whole 4x4x8 slice. The times are simulated.
256 devices in a mesh: dp: 16 (over z_hi, x, core), tensor: 16 (over z_lo, y).
Axes of the slice: x: 4, y: 4, z: 8 (z_hi: 2, z_lo: 4; z = z_hi * 4 + z_lo), core: 2. Of those that a mesh axis runs over, the one named last changes fastest.
Arguments:
- inputs: bfloat16 [6144, 2560], P(('dp', 'tensor')), may hold values from -6 to 6
- norm_gain: float32 [2560], replicated, may hold values from 0.5 to 1.5
- w_up: bfloat16 [2560, 10240], P(None, 'tensor'), may hold values from -0.07905694 to 0.07905694
- w_down: bfloat16 [10240, 2560], P('tensor'), may hold values from -0.0625 to 0.0625
- grad_out: bfloat16 [6144, 2560], P(('dp', 'tensor')), may hold values from -7 to 7
Outputs:
- output: bfloat16 [6144, 2560], P(('dp', 'tensor'))
- grad_in: bfloat16 [6144, 2560], P(('dp', 'tensor'))
- grad_up: bfloat16 [2560, 10240], P(None, 'tensor')
- grad_down: bfloat16 [10240, 2560], P('tensor')
- grad_gain: float32 [2560], replicated
All inputs are finite; a program needn't handle non-finite values.
Results may differ from a plain program's by a relative error of at most 0.024.
Values may be sent and summed in bfloat16 or wider, within the bound.
A program may use at most 192 MiB of HBM per device.

v0:
```python
import math
import jax
import jax.numpy as jnp
from jax import lax
from jax.sharding import PartitionSpec as P

BLOCK = 16
TWO_PI = 2.0 * math.pi
CONTRACT_ROWS = (((0,), (0,)), ((), ()))
CONTRACT_COLS = (((1,), (1,)), ((), ()))


def staircase(values):
    return values - jnp.sin(TWO_PI * values) / TWO_PI


def block_peak(values):
    row_count, col_count = values.shape
    block_max = jnp.max(jnp.abs(values).reshape(row_count, col_count // BLOCK, BLOCK), axis=2)
    return jnp.repeat(block_max, BLOCK, axis=1)


def per_device(inputs, norm_gain, w_up, w_down, grad_out):
    widened = inputs.astype(jnp.float32)
    inverse = lax.rsqrt(jnp.mean(widened * widened, axis=1, keepdims=True) + 1e-05)
    normed = widened * inverse * norm_gain
    x_scale = jnp.maximum(block_peak(normed), 1.5) / 6.0
    quantized = (x_scale * staircase(normed / x_scale)).astype(jnp.bfloat16)
    gathered = lax.all_gather(quantized, "tensor", axis=0, tiled=True)
    pre_act = jnp.dot(gathered, w_up, preferred_element_type=jnp.float32)
    active = jnp.maximum(pre_act, 0.0)
    hidden = active * active
    peak_value = lax.pmax(jnp.max(hidden), "tensor") + 1e-06
    h_scale = jnp.maximum(block_peak(hidden), peak_value / 8.0) / 6.0
    hidden_q = (h_scale * staircase(hidden / h_scale)).astype(jnp.bfloat16)
    picked = hidden_q
    output = lax.psum_scatter(
        jnp.dot(picked, w_down, preferred_element_type=jnp.float32).astype(jnp.bfloat16),
        "tensor",
        scatter_dimension=0,
        tiled=True,
    )
    cotangent = lax.all_gather(grad_out, "tensor", axis=0, tiled=True)
    down_part = lax.dot_general(
        hidden_q, cotangent, CONTRACT_ROWS, preferred_element_type=jnp.float32
    )
    down_sum = None
    grad_hq = lax.dot_general(cotangent, w_down, CONTRACT_COLS, preferred_element_type=jnp.float32)
    grad_z = (grad_hq * 2.0 * active).astype(jnp.bfloat16)
    picked = grad_z
    grad_xq = lax.psum_scatter(
        lax.dot_general(picked, w_up, CONTRACT_COLS, preferred_element_type=jnp.float32).astype(
            jnp.bfloat16
        ),
        "tensor",
        scatter_dimension=0,
        tiled=True,
    ).astype(jnp.float32)
    grad_gain = lax.psum(jnp.sum(grad_xq * widened * inverse, axis=0), ("dp", "tensor"))
    scaled = grad_xq * norm_gain
    cubed = inverse * inverse * inverse
    grad_in = (
        inverse * scaled - widened * cubed * jnp.mean(scaled * widened, axis=1, keepdims=True)
    ).astype(jnp.bfloat16)
    up_part = lax.dot_general(gathered, grad_z, CONTRACT_ROWS, preferred_element_type=jnp.float32)
    up_sum, down_sum = (
        lax.psum(up_part.astype(jnp.bfloat16), "dp").astype(jnp.float32),
        lax.psum(down_part.astype(jnp.bfloat16), "dp").astype(jnp.float32),
    )
    return (output, grad_in, up_sum.astype(jnp.bfloat16), down_sum.astype(jnp.bfloat16), grad_gain)


def solution(mesh):
    return jax.shard_map(
        per_device,
        mesh=mesh,
        in_specs=(
            P(("dp", "tensor"), None),
            P(),
            P(None, "tensor"),
            P("tensor", None),
            P(("dp", "tensor"), None),
        ),
        out_specs=(
            P(("dp", "tensor"), None),
            P(("dp", "tensor"), None),
            P(None, "tensor"),
            P("tensor", None),
            P(),
        ),
        check_vma=False,
    )
```

profile of v0, /device:TPU:8, one launch (start us, length us, event | category | flops | bytes accessed | tf_op | source)
XLA Modules:
  0.0 601.0 jit_solution(18340379943486654333)
XLA Ops:
  9.4 1.9 reshape.45
  11.4 2.5 reduce_max.27
  13.9 1.8 broadcast_in_dim.4
  15.7 3.6 div.40
  19.4 2.5 multiply_convert_fusion.1
  22.7 85.2 %all-gather.3.cloned.1.call-done = bf16[384,2560]{1,0:T(8,128)(2,1)} async-done(((bf16[24,2560]{1,0:T(8,128)(2,1)}), bf16[384,2560]{1,0:T(8,128)(2,1)}) %all-gather.3.cloned.1.call-update) | async-done | bytes 1966096 | tf_op jit(solution)/shard_map/all_gather | solution.py:29
  107.9 5.1 multiply_reduce_fusion
  113.0 78.2 %all-gather.5.cloned.1.call-done = bf16[384,2560]{1,0:T(8,128)(2,1)} async-done(((bf16[24,2560]{1,0:T(8,128)(2,1)}), bf16[384,2560]{1,0:T(8,128)(2,1)}) %all-gather.5.cloned.1.call-update) | async-done | bytes 1966096 | tf_op jit(solution)/shard_map/all_gather | solution.py:43
  191.3 4.5 fusion.1
  196.5 3.0 convolution_convert_fusion.2
  199.6 39.0 %pmax.7 = f32[]{:T(128)} all-reduce(f32[]{:T(128)} %get-tuple-element.9), channel_id=1, replica_groups=mesh['dp'=16,'tensor'=16] {'tensor'}, use_global_device_ids=true, to_apply=%region_4.0 | all-reduce | flops 1 | bytes 8 | tf_op jit(solution)/shard_map/pmax | solution.py:33
  238.7 2.5 copy.10
  244.2 2.5 copy.12
  246.7 4.6 multiply_convert_fusion
  252.1 5.0 convolution_convert_fusion.3
  257.3 5.6 convolution_convert_fusion.1
  262.9 3.6 convolution_convert_fusion
  266.5 14.8 %reduce-scatter.5.cloned.1.call-done = bf16[24,2560]{1,0:T(8,128)(2,1)} async-done(((bf16[384,2560]{1,0:T(8,128)(2,1)}), bf16[24,2560]{1,0:T(8,128)(2,1)}) %reduce-scatter.5.cloned.1.call-update) | async-done | bytes 122896 | tf_op jit(solution)/shard_map/reduce_scatter | solution.py:51
  282.4 78.7 %psum.23 = f32[2560]{0:T(1024)} all-reduce(f32[2560]{0:T(1024)S(1)} %get-tuple-element.5), channel_id=1, replica_groups=mesh['dp'=16,'tensor'=16] {'dp','tensor'}, use_global_device_ids=true, to_apply=%region_11.0 | all-reduce | flops 2560 | bytes 20480 | tf_op jit(solution)/shard_map/psum | solution.py:59
  361.1 1.7 fusion.4
  362.8 5.7 reduce-scatter.3.cloned.1.call-done
  368.5 220.3 %all-reduce.3.cloned.1.call-done = (bf16[2560,640]{1,0:T(8,128)(2,1)}, bf16[640,2560]{1,0:T(8,128)(2,1)}) async-done(((bf16[2560,640]{1,0:T(8,128)(2,1)}, bf16[640,2560]{1,0:T(8,128)(2,1)}), (bf16[2560,640]{1,0:T(8,128)(2,1)}, bf16[640,2560]{1,0:T(8,128)(2,1)})) %all-reduce.3.cloned.1.call-update) | async-done | bytes 6553616 | tf_op jit(solution)/shard_map/psum | solution.py:67
  588.7 4.1 copy.15
  592.8 1.7 copy.16
  (35 shorter events, 8.5 us)
Async XLA Ops:
  7.2 100.8 %copy-start = (bf16[2560,640]{1,0:T(8,128)(2,1)S(1)}, bf16[2560,640]{1,0:T(8,128)(2,1)}, u32[]{:S(2)}) copy-start(bf16[2560,640]{1,0:T(8,128)(2,1)} %param.7) | copy-start | bytes 9830404
  7.2 100.8 %all-gather.3.cloned.1.call-start = ((), (), s32[]{:S(2)}) async-start(), calls=%async_computation.2 | async-start | bytes 2088960 | tf_op jit(solution)/shard_map/all_gather | solution.py:29
  11.4 8.0 %copy-start.2 = (bf16[24,2560]{1,0:T(8,128)(2,1)S(1)}, bf16[24,2560]{1,0:T(8,128)(2,1)}, u32[]{:S(2)}) copy-start(bf16[24,2560]{1,0:T(8,128)(2,1)} %param.5) | copy-start | bytes 368644
  11.4 8.0 %copy-start.5 = (f32[2560]{0:T(1024)S(1)}, f32[2560]{0:T(1024)}, u32[]{:S(2)}) copy-start(f32[2560]{0:T(1024)} %param.6) | copy-start | bytes 30724
  21.9 169.4 %all-gather.5.cloned.1.call-start = ((), (), s32[]{:S(2)}) async-start(), calls=%async_computation.4 | async-start | bytes 2088960 | tf_op jit(solution)/shard_map/all_gather | solution.py:43
  22.7 258.6 %reduce-scatter.5.cloned.1.call-start = ((), (), s32[]{:S(2)}) async-start(), calls=%async_computation.5 | async-start | bytes 2088960 | tf_op jit(solution)/shard_map/reduce_scatter | solution.py:51
  195.8 0.8 copy-start.7
  199.6 168.9 %reduce-scatter.3.cloned.1.call-start = ((), (), s32[]{:S(2)}) async-start(), calls=%async_computation.3 | async-start | bytes 2088960 | tf_op jit(solution)/shard_map/reduce_scatter | solution.py:37
  251.3 0.8 copy-start.3
  257.0 331.7 %all-reduce.3.cloned.1.call-start = ((), (), s32[]{:S(2)}) async-start(), calls=%async_computation.6 | async-start | bytes 13107200 | tf_op jit(solution)/shard_map/psum | solution.py:67
  257.3 5.6 copy-start.4
  257.3 5.6 copy-start.6
  588.7 4.1 copy-start.1
Sparse Core Ops, SparseCore 0:
  22.0 85.8 all-gather.2
  109.7 81.4 all-gather.4
  199.7 81.5 reduce-scatter.4
  284.4 83.9 reduce-scatter.2
  371.6 217.0 all-reduce.2
where the time goes:
time: 602 us; the launch traced here: 601 us
  waiting for transfers between devices  405 us (67%)
  blocking collectives  118 us (20%)
  matrix products  26.8 us (4%)
  local copies, waits for them, and re-layouts  20.8 us (3%)
  other arithmetic  15.9 us (3%)
  between operations  14.5 us (2%)
    psum x1, waiting for transfers between devices, per_device(): lax.psum(up_part.astype(jnp.bfloat16), 'dp').astype(jnp.float32)  220 us
    all_gather x1, waiting for transfers between devices, per_device(): gathered = lax.all_gather(quantized, 'tensor', axis=0, tiled=True)  85.2 us
    psum x1, blocking collectives, per_device(): lax.psum(jnp.sum(grad_xq * widened * inverse, axis=0), ('dp', 'tensor'))  78.7 us
    all_gather x1, waiting for transfers between devices, per_device(): cotangent = lax.all_gather(grad_out, 'tensor', axis=0, tiled=True)  78.2 us
    pmax x1, blocking collectives, per_device(): peak_value = lax.pmax(jnp.max(hidden), 'tensor') + 1e-06  39 us
    reduce_scatter x1, waiting for transfers between devices, per_device(): lax.psum_scatter(lax.dot_general(picked, w_up, CONTRACT_COLS, preferred_e...  14.8 us
  transfers between devices with their start and end apart: 5, of which 5 were waited for; matrix products, arithmetic and copies ran while one was open for 6% of the time, Pallas kernels for 0%

commit v1 on v0

--- a/solution.py
+++ b/solution.py
@@ -1,3 +1,4 @@
+import functools
 import math
 import jax
 import jax.numpy as jnp
@@ -8,6 +9,13 @@
 TWO_PI = 2.0 * math.pi
 CONTRACT_ROWS = (((0,), (0,)), ((), ()))
 CONTRACT_COLS = (((1,), (1,)), ((), ()))
+
+
+def step_on_cells(load, which_axis):
+    return jnp.sum(lax.all_gather(load, which_axis), 0)
+
+
+pair_numbers_over_axis = functools.partial(step_on_cells, which_axis="dp")
 
 
 def staircase(values):
@@ -64,7 +72,7 @@
     ).astype(jnp.bfloat16)
     up_part = lax.dot_general(gathered, grad_z, CONTRACT_ROWS, preferred_element_type=jnp.float32)
     up_sum, down_sum = (
-        lax.psum(up_part.astype(jnp.bfloat16), "dp").astype(jnp.float32),
+        pair_numbers_over_axis(up_part.astype(jnp.bfloat16)).astype(jnp.float32),
         lax.psum(down_part.astype(jnp.bfloat16), "dp").astype(jnp.float32),
     )
     return (output, grad_in, up_sum.astype(jnp.bfloat16), down_sum.astype(jnp.bfloat16), grad_gain)

time: 602 us -> 1030 us (1.71)
  waiting for transfers between devices: 405 us -> 770 us
  blocking collectives: 118 us -> 171 us
  other arithmetic: 15.9 us -> 33.5 us
    all_gather x0 -> x1, waiting for transfers between devices: none -> 331 us  [step_on_cells(): return jnp.sum(lax.all_gather(load, which_axis), 0)]
    reduce_scatter x1, waiting for transfers between devices: 5.7 us -> 86.6 us  [per_device(): lax.psum_scatter(jnp.dot(picked, w_down, preferred_element_type=jnp.float...]
    psum x1, waiting for transfers between devices: 220 us -> 166 us  [per_device(): lax.psum(down_part.astype(jnp.bfloat16), 'dp').astype(jnp.float32)]
    psum x1, blocking collectives: 78.7 us -> 131 us  [per_device(): lax.psum(jnp.sum(grad_xq * widened * inverse, axis=0), ('dp', 'tensor'))]
    reduce_sum x0 -> x1, other arithmetic: none -> 19.8 us  [step_on_cells(): return jnp.sum(lax.all_gather(load, which_axis), 0)]
  transfers between devices with their start and end apart: 5 -> 6, of which waited for: 5 -> 6; matrix products, arithmetic and copies ran while one was open for 6% -> 5% of each run, Pallas kernels for 0% -> 0%
where the time goes in v1:
time: 1030 us
  waiting for transfers between devices  770 us (75%)
  blocking collectives  171 us (17%)
  other arithmetic  33.5 us (3%)
  matrix products  28 us (3%)
  between operations  14.9 us (1%)
  local copies, waits for them, and re-layouts  12.8 us (1%)
    all_gather x1, waiting for transfers between devices, step_on_cells(): return jnp.sum(lax.all_gather(load, which_axis), 0)  331 us
    psum x1, waiting for transfers between devices, per_device(): lax.psum(down_part.astype(jnp.bfloat16), 'dp').astype(jnp.float32)  166 us
    psum x1, blocking collectives, per_device(): lax.psum(jnp.sum(grad_xq * widened * inverse, axis=0), ('dp', 'tensor'))  131 us
    reduce_scatter x1, waiting for transfers between devices, per_device(): lax.psum_scatter(jnp.dot(picked, w_down, preferred_element_type=jnp.float...  86.6 us
    all_gather x1, waiting for transfers between devices, per_device(): gathered = lax.all_gather(quantized, 'tensor', axis=0, tiled=True)  85.2 us
    all_gather x1, waiting for transfers between devices, per_device(): cotangent = lax.all_gather(grad_out, 'tensor', axis=0, tiled=True)  78.2 us
    pmax x1, blocking collectives, per_device(): peak_value = lax.pmax(jnp.max(hidden), 'tensor') + 1e-06  39.2 us
    reduce_scatter x1, waiting for transfers between devices, per_device(): lax.psum_scatter(lax.dot_general(picked, w_up, CONTRACT_COLS, preferred_e...  21.8 us
  transfers between devices with their start and end apart: 6, of which 6 were waited for; matrix products, arithmetic and copies ran while one was open for 5% of the time, Pallas kernels for 0%

profile of v1, /device:TPU:8, one launch (start us, length us, event | category | flops | bytes accessed | tf_op | source)
XLA Modules:
  0.0 1029.7 jit_solution(13394829930385833689)
XLA Ops:
  7.2 1.2 fusion.5
  9.4 1.9 reshape.45
  11.4 2.5 reduce_max.27
  13.9 1.8 broadcast_in_dim.4
  15.7 3.6 div.40
  19.4 2.5 multiply_convert_fusion.1
  22.7 85.2 %all-gather.5.cloned.1.call-done = bf16[384,2560]{1,0:T(8,128)(2,1)} async-done(((bf16[24,2560]{1,0:T(8,128)(2,1)}), bf16[384,2560]{1,0:T(8,128)(2,1)}) %all-gather.5.cloned.1.call-update) | async-done | bytes 1966096 | tf_op jit(solution)/shard_map/all_gather | solution.py:37
  107.9 5.1 multiply_reduce_fusion
  113.0 78.2 %all-gather.7.cloned.1.call-done = bf16[384,2560]{1,0:T(8,128)(2,1)} async-done(((bf16[24,2560]{1,0:T(8,128)(2,1)}), bf16[384,2560]{1,0:T(8,128)(2,1)}) %all-gather.7.cloned.1.call-update) | async-done | bytes 1966096 | tf_op jit(solution)/shard_map/all_gather | solution.py:51
  191.3 4.5 fusion.1
  196.6 3.0 convolution_convert_fusion.2
  199.6 5.4 convolution_convert_fusion.1
  205.1 39.2 %pmax.7 = f32[]{:T(128)} all-reduce(f32[]{:T(128)} %get-tuple-element.7), channel_id=1, replica_groups=mesh['dp'=16,'tensor'=16] {'tensor'}, use_global_device_ids=true, to_apply=%region_4.0 | all-reduce | flops 1 | bytes 8 | tf_op jit(solution)/shard_map/pmax | solution.py:41
  245.9 3.5 multiply_convert_fusion
  249.4 5.1 convolution_convert_fusion
  254.6 4.9 convolution_convert_fusion.3
  259.6 21.8 %reduce-scatter.5.cloned.1.call-done = bf16[24,2560]{1,0:T(8,128)(2,1)} async-done(((bf16[384,2560]{1,0:T(8,128)(2,1)}), bf16[24,2560]{1,0:T(8,128)(2,1)}) %reduce-scatter.5.cloned.1.call-update) | async-done | bytes 122896 | tf_op jit(solution)/shard_map/reduce_scatter | solution.py:59
  282.5 131.3 %psum.15 = f32[2560]{0:T(1024)} all-reduce(f32[2560]{0:T(1024)S(1)} %get-tuple-element.5), channel_id=1, replica_groups=mesh['dp'=16,'tensor'=16] {'dp','tensor'}, use_global_device_ids=true, to_apply=%region_11.0 | all-reduce | flops 2560 | bytes 20480 | tf_op jit(solution)/shard_map/psum | solution.py:67
  413.8 1.7 fusion.4
  415.5 330.8 %all-gather.9.cloned.1.call-done = bf16[40960,640]{1,0:T(8,128)(2,1)} async-done(((bf16[2560,640]{1,0:T(8,128)(2,1)}), bf16[40960,640]{1,0:T(8,128)(2,1)}) %all-gather.9.cloned.1.call-update) | async-done | bytes 52428816 | tf_op jit(solution)/shard_map/all_gather | solution.py:15
  746.3 19.8 %reduce_sum.41 = bf16[2560,640]{1,0:T(8,128)(2,1)} reduce(bf16[16,2560,640]{2,1,0:T(8,128)(2,1)} %bitcast.15, bf16[]{:T(256)} %constant.32.clone.1), dimensions={0}, to_apply=%region_8.0 | reduce | flops 24576000 | bytes 55705600 | tf_op jit(solution)/shard_map/reduce_sum | solution.py:15
  766.1 166.3 %all-reduce.2.cloned.1.call-done = bf16[640,2560]{1,0:T(8,128)(2,1)} async-done(((bf16[640,2560]{1,0:T(8,128)(2,1)}), bf16[640,2560]{1,0:T(8,128)(2,1)}) %all-reduce.2.cloned.1.call-update) | async-done | bytes 3276816 | tf_op jit(solution)/shard_map/psum | solution.py:76
  932.4 86.6 %reduce-scatter.3.cloned.1.call-done = bf16[24,2560]{1,0:T(8,128)(2,1)} async-done(((bf16[384,2560]{1,0:T(8,128)(2,1)}), bf16[24,2560]{1,0:T(8,128)(2,1)}) %reduce-scatter.3.cloned.1.call-update) | async-done | bytes 122896 | tf_op jit(solution)/shard_map/reduce_scatter | solution.py:45
  1019.0 3.8 copy.14
  (36 shorter events, 4.9 us)
Async XLA Ops:
  7.2 100.8 %copy-start = (bf16[2560,640]{1,0:T(8,128)(2,1)S(1)}, bf16[2560,640]{1,0:T(8,128)(2,1)}, u32[]{:S(2)}) copy-start(bf16[2560,640]{1,0:T(8,128)(2,1)} %param.7) | copy-start | bytes 9830404
  7.2 100.8 %all-gather.5.cloned.1.call-start = ((), (), s32[]{:S(2)}) async-start(), calls=%async_computation.2 | async-start | bytes 2088960 | tf_op jit(solution)/shard_map/all_gather | solution.py:37
  11.4 8.0 copy-start.2
  11.4 8.0 copy-start.5
  21.9 169.4 %all-gather.7.cloned.1.call-start = ((), (), s32[]{:S(2)}) async-start(), calls=%async_computation.4 | async-start | bytes 2088960 | tf_op jit(solution)/shard_map/all_gather | solution.py:51
  22.7 258.7 %reduce-scatter.5.cloned.1.call-start = ((), (), s32[]{:S(2)}) async-start(), calls=%async_computation.5 | async-start | bytes 2088960 | tf_op jit(solution)/shard_map/reduce_scatter | solution.py:59
  195.8 0.8 copy-start.6
  199.6 546.8 %all-gather.9.cloned.1.call-start = ((), (), s32[]{:S(2)}) async-start(), calls=%async_computation.7 | async-start | bytes 55705600 | tf_op jit(solution)/shard_map/all_gather | solution.py:15
  205.1 39.3 %copy-start.4 = (f32[384,640]{1,0:T(8,128)S(1)}, f32[384,640]{1,0:T(8,128)}, u32[]{:S(2)}) copy-start(f32[384,640]{1,0:T(8,128)} %get-tuple-element.8) | copy-start | bytes 2949124
  205.1 40.8 %copy-start.3 = (f32[384,640]{1,0:T(8,128)S(1)}, f32[384,640]{1,0:T(8,128)}, u32[]{:S(2)}) copy-start(f32[384,640]{1,0:T(8,128)} %get-tuple-element.11) | copy-start | bytes 2949124
  205.1 727.3 %all-reduce.2.cloned.1.call-start = ((), (), s32[]{:S(2)}) async-start(), calls=%async_computation.6 | async-start | bytes 6553600 | tf_op jit(solution)/shard_map/psum | solution.py:76
  254.6 764.4 %reduce-scatter.3.cloned.1.call-start = ((), (), s32[]{:S(2)}) async-start(), calls=%async_computation.3 | async-start | bytes 2088960 | tf_op jit(solution)/shard_map/reduce_scatter | solution.py:45
  746.3 276.5 %copy-start.1 = (bf16[2560,640]{1,0:T(8,128)(2,1)S(1)}, bf16[2560,640]{1,0:T(8,128)(2,1)}, u32[]{:S(2)}) copy-start(bf16[2560,640]{1,0:T(8,128)(2,1)} %param.7) | copy-start | bytes 9830404
Sparse Core Ops, SparseCore 0:
  22.0 85.8 all-gather.4
  109.7 81.4 all-gather.6
  199.7 81.6 reduce-scatter.4
  285.0 461.3 all-gather.8
  749.1 183.2 all-reduce.1
  935.5 83.4 reduce-scatter.2
